TPU v7x, 512 devices: a whole 4x8x8 slice. The times are simulated.
512 devices in a mesh: head: 8 (over x, z_lo), blk: 64 (over y, z_hi, core).
Axes of the slice: x: 4, y: 8, z: 8 (z_hi: 4, z_lo: 2; z = z_hi * 2 + z_lo), core: 2. Of those that a mesh axis runs over, the one named last changes fastest.
Arguments:
- queries: bfloat16 [65536, 2048], P(('blk', 'head')), may hold values from -4 to 4
- keys: bfloat16 [65536, 2048], P(('blk', 'head')), may hold values from -4 to 4
- values: bfloat16 [65536, 2048], P(('blk', 'head')), may hold values from -6 to 6
- outputs: bfloat16 [65536, 2048], P(('blk', 'head')), may hold values from -6 to 6
- out_grad: bfloat16 [65536, 2048], P(('blk', 'head')), may hold values from -96 to 96
- log_sum: float32 [65536, 16], P(('blk', 'head')), may hold values from 7 to 9
Outputs:
- query_grad: bfloat16 [65536, 2048], P(('blk', 'head'))
- key_grad: bfloat16 [65536, 2048], P(('blk', 'head'))
- value_grad: bfloat16 [65536, 2048], P(('blk', 'head'))
All inputs are finite; a program needn't handle non-finite values.
Results may differ from a plain program's by a relative error of at most 0.0053.
Values may be sent and summed in bfloat16 or wider, within the bound.
A program may use at most 64 MiB of HBM per device.

v0:
```python
import jax
import jax.numpy as jnp
from jax import lax
from jax.sharding import PartitionSpec as P

HD = 128
REACH = 1
SPAN = 512


def padded(cells, sides, width):
    for axis, dim in sides:
        count = lax.axis_size(axis)
        head = lax.slice_in_dim(cells, 0, width, axis=dim)
        tail = lax.slice_in_dim(cells, cells.shape[dim] - width, cells.shape[dim], axis=dim)
        cells = jnp.concatenate(
            [
                lax.ppermute(tail, axis, [(i, (i + 1) % count) for i in range(count)]),
                cells,
                lax.ppermute(head, axis, [((i + 1) % count, i) for i in range(count)]),
            ],
            axis=dim,
        )
    return cells


def from_behind(shard, axis, by):
    length = lax.axis_size(axis)
    return lax.ppermute(shard, axis, [(i, (i + by) % length) for i in range(length)])


def block_terms(query_rows, grad_rows, lse_rows, delta_rows, key_rows, value_rows):
    softmax_scale = HD ** (-0.5)
    score_matrix = (
        jnp.einsum("qhd,khd->hqk", query_rows, key_rows, preferred_element_type=jnp.float32)
        * softmax_scale
    )
    attend = jnp.exp(score_matrix - jnp.transpose(lse_rows)[:, :, None])
    weights_reduced = attend.astype(jnp.bfloat16)
    value_portion = jnp.einsum(
        "hqk,qhd->khd", weights_reduced, grad_rows, preferred_element_type=jnp.float32
    )
    weights_gradient = jnp.einsum(
        "qhd,khd->hqk", grad_rows, value_rows, preferred_element_type=jnp.float32
    )
    logits_gradient = (attend * (weights_gradient - jnp.transpose(delta_rows)[:, :, None])).astype(
        jnp.bfloat16
    )
    query_part = (
        jnp.einsum("hqk,khd->qhd", logits_gradient, key_rows, preferred_element_type=jnp.float32)
        * softmax_scale
    )
    key_portion = (
        jnp.einsum("hqk,qhd->khd", logits_gradient, query_rows, preferred_element_type=jnp.float32)
        * softmax_scale
    )
    return (query_part, key_portion, value_portion)


def per_device(queries, keys, values, outputs, out_grad, log_sum):
    groups = lax.axis_size("head")
    local_rows = queries.shape[0] * groups
    local_heads = queries.shape[1] // groups // HD
    span = SPAN
    rim = REACH * span
    window = (2 * REACH + 1) * span
    count = local_rows // span

    def split_heads(array):
        return array.reshape(local_rows, local_heads, HD)

    moved = (
        lax.all_to_all(queries, "head", split_axis=1, concat_axis=0, tiled=True),
        lax.all_to_all(keys, "head", split_axis=1, concat_axis=0, tiled=True),
        lax.all_to_all(values, "head", split_axis=1, concat_axis=0, tiled=True),
        lax.all_to_all(outputs, "head", split_axis=1, concat_axis=0, tiled=True),
        lax.all_to_all(out_grad, "head", split_axis=1, concat_axis=0, tiled=True),
    )
    lse_local = lax.all_to_all(log_sum, "head", split_axis=1, concat_axis=0, tiled=True)
    query_h = split_heads(moved[0])
    key_h = split_heads(moved[1])
    value_h = split_heads(moved[2])
    output_h = split_heads(moved[3])
    grad_h = split_heads(moved[4])
    delta_local = jnp.sum(grad_h.astype(jnp.float32) * output_h.astype(jnp.float32), axis=2)
    paired = jnp.concatenate((key_h, value_h), axis=1)
    widened = padded(paired, (("blk", 0),), rim)
    extended = jnp.zeros((local_rows + 2 * rim, 2 * local_heads, HD), jnp.float32)
    query_pieces = []
    for block in range(count):
        start = block * span
        query_part, key_portion, value_portion = block_terms(
            query_h[start : start + span],
            grad_h[start : start + span],
            lse_local[start : start + span],
            delta_local[start : start + span],
            widened[start : start + window, :local_heads],
            widened[start : start + window, local_heads:],
        )
        query_pieces.append(query_part)
        extended = extended.at[start : start + window].add(
            jnp.concatenate((key_portion, value_portion), axis=1)
        )
    query_total = jnp.concatenate(query_pieces, axis=0)
    from_next = from_behind(extended[:rim], "blk", -1)
    from_prev = from_behind(extended[rim + local_rows :], "blk", 1)
    inner = extended[rim : rim + local_rows]
    inner = inner.at[:rim].add(from_prev)
    inner = inner.at[local_rows - rim :].add(from_next)
    key_total = inner[:, :local_heads]
    value_total = inner[:, local_heads:]

    def merge_heads(array):
        return array.astype(jnp.bfloat16).reshape(local_rows, local_heads * HD)

    return (
        lax.all_to_all(merge_heads(query_total), "head", split_axis=0, concat_axis=1, tiled=True),
        lax.all_to_all(merge_heads(key_total), "head", split_axis=0, concat_axis=1, tiled=True),
        lax.all_to_all(merge_heads(value_total), "head", split_axis=0, concat_axis=1, tiled=True),
    )


def solution(mesh):
    in_specs = (
        P(("blk", "head"), None),
        P(("blk", "head"), None),
        P(("blk", "head"), None),
        P(("blk", "head"), None),
        P(("blk", "head"), None),
        P(("blk", "head"), None),
    )
    out_specs = (P(("blk", "head"), None), P(("blk", "head"), None), P(("blk", "head"), None))
    return jax.shard_map(
        per_device, mesh=mesh, in_specs=in_specs, out_specs=out_specs, check_vma=False
    )
```

profile of v0, /device:TPU:1, one launch (start us, length us, event | category | flops | bytes accessed | tf_op | source)
XLA Modules:
  0.0 177.0 jit_solution(2294173496364865562)
XLA Ops:
  0.6 6.8 %all-to-all-start.3 = ((f32[128,8,2]{0,2,1:T(2,128)}), f32[128,8,2]{0,2,1:T(2,128)S(1)}, u32[]{:S(2)}, u32[]{:S(2)}) async-start(f32[128,8,2]{0,2,1:T(2,128)} %bitcast.93), calls=%async_computation.3 | async-start | bytes 16384 | tf_op jit(solution)/shard_map/all_to_all | solution.py:79
  7.4 2.1 %copy.85 = bf16[128,2048]{0,1:T(8,128)(2,1)} copy(bf16[128,2048]{1,0:T(8,128)(2,1)} %param.15) | data formatting | bytes 1048576 | tf_op args[1]
  9.5 2.9 %all-to-all-done.3 = f32[128,8,2]{0,2,1:T(2,128)S(1)} async-done(((f32[128,8,2]{0,2,1:T(2,128)}), f32[128,8,2]{0,2,1:T(2,128)S(1)}, u32[]{:S(2)}, u32[]{:S(2)}) %all-to-all-start.3) | async-done | bytes 8224 | tf_op jit(solution)/shard_map/all_to_all | solution.py:79
  12.5 3.5 %all-to-all-start = ((bf16[128,8,256]{0,2,1:T(8,128)(2,1)}), bf16[128,8,256]{0,2,1:T(8,128)(2,1)S(1)}, u32[]{:S(2)}, u32[]{:S(2)}) async-start(bf16[128,8,256]{0,2,1:T(8,128)(2,1)} %bitcast), calls=%async_computation | async-start | bytes 1048576 | tf_op jit(solution)/shard_map/all_to_all | solution.py:74
  16.0 2.1 %copy.87 = bf16[128,2048]{0,1:T(8,128)(2,1)} copy(bf16[128,2048]{1,0:T(8,128)(2,1)} %param.16) | data formatting | bytes 1048576 | tf_op args[2]
  18.1 5.4 %all-to-all-done = bf16[128,8,256]{0,2,1:T(8,128)(2,1)S(1)} async-done(((bf16[128,8,256]{0,2,1:T(8,128)(2,1)}), bf16[128,8,256]{0,2,1:T(8,128)(2,1)S(1)}, u32[]{:S(2)}, u32[]{:S(2)}) %all-to-all-start) | async-done | bytes 524320 | tf_op jit(solution)/shard_map/all_to_all | solution.py:74
  23.5 3.5 %all-to-all-start.1 = ((bf16[128,8,256]{0,2,1:T(8,128)(2,1)}), bf16[128,8,256]{0,2,1:T(8,128)(2,1)S(1)}, u32[]{:S(2)}, u32[]{:S(2)}) async-start(bf16[128,8,256]{0,2,1:T(8,128)(2,1)} %bitcast.2), calls=%async_computation.1 | async-start | bytes 1048576 | tf_op jit(solution)/shard_map/all_to_all | solution.py:75
  27.8 6.6 %all-to-all-done.1 = bf16[128,8,256]{0,2,1:T(8,128)(2,1)S(1)} async-done(((bf16[128,8,256]{0,2,1:T(8,128)(2,1)}), bf16[128,8,256]{0,2,1:T(8,128)(2,1)S(1)}, u32[]{:S(2)}, u32[]{:S(2)}) %all-to-all-start.1) | async-done | bytes 524320 | tf_op jit(solution)/shard_map/all_to_all | solution.py:75
  34.4 3.5 %all-to-all-start.5 = ((bf16[128,8,256]{2,0,1:T(8,128)(2,1)}), bf16[128,8,256]{2,0,1:T(8,128)(2,1)S(1)}, u32[]{:S(2)}, u32[]{:S(2)}) async-start(bf16[128,8,256]{2,0,1:T(8,128)(2,1)} %bitcast.72), calls=%async_computation.5 | async-start | bytes 1048576 | tf_op jit(solution)/shard_map/all_to_all | solution.py:76
  38.8 6.6 %all-to-all-done.5 = bf16[128,8,256]{2,0,1:T(8,128)(2,1)S(1)} async-done(((bf16[128,8,256]{2,0,1:T(8,128)(2,1)}), bf16[128,8,256]{2,0,1:T(8,128)(2,1)S(1)}, u32[]{:S(2)}, u32[]{:S(2)}) %all-to-all-start.5) | async-done | bytes 524320 | tf_op jit(solution)/shard_map/all_to_all | solution.py:76
  46.2 3.5 %all-to-all-start.4 = ((bf16[128,8,256]{2,0,1:T(8,128)(2,1)}), bf16[128,8,256]{2,0,1:T(8,128)(2,1)S(1)}, u32[]{:S(2)}, u32[]{:S(2)}) async-start(bf16[128,8,256]{2,0,1:T(8,128)(2,1)} %bitcast.73), calls=%async_computation.4 | async-start | bytes 1048576 | tf_op jit(solution)/shard_map/all_to_all | solution.py:77
  50.5 6.6 %all-to-all-done.4 = bf16[128,8,256]{2,0,1:T(8,128)(2,1)S(1)} async-done(((bf16[128,8,256]{2,0,1:T(8,128)(2,1)}), bf16[128,8,256]{2,0,1:T(8,128)(2,1)S(1)}, u32[]{:S(2)}, u32[]{:S(2)}) %all-to-all-start.4) | async-done | bytes 524320 | tf_op jit(solution)/shard_map/all_to_all | solution.py:77
  57.2 3.5 %all-to-all-start.2 = ((bf16[128,8,256]{2,0,1:T(8,128)(2,1)}), bf16[128,8,256]{2,0,1:T(8,128)(2,1)S(1)}, u32[]{:S(2)}, u32[]{:S(2)}) async-start(bf16[128,8,256]{2,0,1:T(8,128)(2,1)} %bitcast.74), calls=%async_computation.2 | async-start | bytes 1048576 | tf_op jit(solution)/shard_map/all_to_all | solution.py:73
  62.4 1.1 fusion.24
  63.6 11.4 %collective-permute-start.1 = (bf16[512,4,128]{2,0,1:T(8,128)(2,1)}, bf16[512,4,128]{2,0,1:T(8,128)(2,1)}, u32[]{:S(2)}, u32[]{:S(2)}) collective-permute-start(bf16[512,4,128]{2,0,1:T(8,128)(2,1)} %get-tuple-element.63), channel_id=1, source_target_pairs={{1,0},{2,1},{3,2},{4,3},{5,4},{6,5},{7,6},{8,7},{9,8},{10,9},{11,1... | collective-permute-start | bytes 1572872 | tf_op jit(solution)/shard_map/ppermute | solution.py:20
  75.0 1.1 bitcast_multiply_fusion
  76.9 1.0 slice.181
  78.0 1.5 reshape.189
  79.5 2.4 %reduce_sum.9 = f32[1024,2]{1,0:T(8,128)S(1)} reduce(f32[1024,2,128]{2,1,0:T(2,128)} %reshape.189, f32[]{:T(128)} %constant.98.clone.1), dimensions={2}, to_apply=%region_0.0 | reduce | flops 260096 | bytes 1056772 | tf_op jit(solution)/shard_map/reduce_sum | solution.py:85
  82.4 5.9 %collective-permute-start = (bf16[512,4,128]{2,0,1:T(8,128)(2,1)}, bf16[512,4,128]{2,0,1:T(8,128)(2,1)S(1)}, u32[]{:S(2)}, u32[]{:S(2)}) collective-permute-start(bf16[512,4,128]{2,0,1:T(8,128)(2,1)} %get-tuple-element.62), channel_id=1, source_target_pairs={{0,1},{1,2},{2,3},{3,4},{4,5},{5,6},{6,7},{7,8},{8,9},{9,10},{10,1... | collective-permute-start | bytes 1572872 | tf_op jit(solution)/shard_map/ppermute | solution.py:18
  88.3 1.9 %collective-permute-done.1 = bf16[512,4,128]{2,0,1:T(8,128)(2,1)} collective-permute-done((bf16[512,4,128]{2,0,1:T(8,128)(2,1)}, bf16[512,4,128]{2,0,1:T(8,128)(2,1)}, u32[]{:S(2)}, u32[]{:S(2)}) %collective-permute-start.1) | collective-permute-done | bytes 524320 | tf_op jit(solution)/shard_map/ppermute | solution.py:20
  90.3 1.9 %fusion.28 = f32[2,1536,512]{2,1,0:T(8,128)S(1)} fusion(bf16[512,2,128]{2,1,0:T(2,128)(2,1)S(1)} %slice.191, bf16[512,4,128]{2,0,1:T(8,128)(2,1)} %collective-permute-done.1, bf16[1024,2,128]{2,0,1:T(8,128)(2,1)S(1)} %copy.90, bf16[1024,2,128]{2,0,1:T(8,128)(2,1)S(1)} %copy.89), kind=kOutput, calls=%fused_computation.46 | convolution fusion | flops 407371776 | bytes 8126464 | tf_op jit(solution)/shard_map/qhd,khd->hqk/dot_general | solution.py:35
  92.2 2.6 %multiply_convert_fusion = bf16[2,1536,512]{2,1,0:T(8,128)(2,1)S(1)} fusion(f32[2,1536,512]{2,1,0:T(8,128)S(1)} %fusion.28, f32[2,512]{1,0:T(2,128)S(1)} %bitcast.95, f32[2,512]{1,0:T(2,128)S(1)} %get-tuple-element.71, bf16[512,2,128]{2,1,0:T(2,128)(2,1)S(1)} %slice.196, bf16[512,4,128]{2,0,1:T(8,128)(2,1)} %collective-permute-done.1, ...), kind=kOutput, calls=%fused_computation | convolution fusion | flops 415236096 | bytes 11280384 | tf_op jit(solution)/shard_map/qhd,khd->hqk/dot_general | solution.py:43
  94.8 1.0 fusion.12
  95.8 1.1 fusion.16
  96.9 1.0 fusion.33
  97.9 1.1 fusion.13
  99.1 1.6 multiply_convert_fusion.1
  100.7 1.0 fusion.11
  102.2 1.0 slice.218
  103.2 4.3 %collective-permute-start.2 = (f32[512,4,128]{2,0,1:T(8,128)}, f32[512,4,128]{2,0,1:T(8,128)}, u32[]{:S(2)}, u32[]{:S(2)}) collective-permute-start(f32[512,4,128]{2,0,1:T(8,128)} %slice.218), channel_id=1, source_target_pairs={{0,1},{1,2},{2,3},{3,4},{4,5},{5,6},{6,7},{7,8},{8,9},{9,10},{10,1... | collective-permute-start | bytes 3145736 | tf_op jit(solution)/shard_map/ppermute | solution.py:29
  107.6 1.1 fusion.21
  108.6 8.2 %collective-permute-start.3 = (f32[512,4,128]{2,0,1:T(8,128)}, f32[512,4,128]{2,0,1:T(8,128)}, u32[]{:S(2)}, u32[]{:S(2)}) collective-permute-start(f32[512,4,128]{2,0,1:T(8,128)} %fusion.21), channel_id=1, source_target_pairs={{0,63},{1,0},{2,1},{3,2},{4,3},{5,4},{6,5},{7,6},{8,7},{9,8},{10,9... | collective-permute-start | bytes 3145736 | tf_op jit(solution)/shard_map/ppermute | solution.py:29
  116.8 1.8 fusion.20
  120.2 2.0 %copy.101 = bf16[1024,256]{1,0:T(8,128)(2,1)} copy(bf16[1024,256]{0,1:T(8,128)(2,1)} %pad_maximum_fusion.3) | data formatting | bytes 1048576 | tf_op jit(solution)/shard_map/concatenate | solution.py:104
  122.2 4.6 %all-to-all-start.6 = ((bf16[8,128,256]{2,1,0:T(8,128)(2,1)}), bf16[8,128,256]{2,1,0:T(8,128)(2,1)}, u32[]{:S(2)}, u32[]{:S(2)}) async-start(bf16[8,128,256]{2,1,0:T(8,128)(2,1)} %bitcast.79), calls=%async_computation.6 | async-start | bytes 1048576 | tf_op jit(solution)/shard_map/all_to_all | solution.py:117
  127.0 1.3 fusion.23
  128.3 15.5 %collective-permute-done.3 = f32[512,4,128]{2,0,1:T(8,128)} collective-permute-done((f32[512,4,128]{2,0,1:T(8,128)}, f32[512,4,128]{2,0,1:T(8,128)}, u32[]{:S(2)}, u32[]{:S(2)}) %collective-permute-start.3) | collective-permute-done | bytes 1048608 | tf_op jit(solution)/shard_map/ppermute | solution.py:29
  143.8 1.4 fusion.22
  146.7 4.5 %all-to-all-done.6 = bf16[8,128,256]{2,1,0:T(8,128)(2,1)} async-done(((bf16[8,128,256]{2,1,0:T(8,128)(2,1)}), bf16[8,128,256]{2,1,0:T(8,128)(2,1)}, u32[]{:S(2)}, u32[]{:S(2)}) %all-to-all-start.6) | async-done | bytes 524320 | tf_op jit(solution)/shard_map/all_to_all | solution.py:117
  151.2 3.5 %all-to-all-start.8 = ((bf16[8,128,256]{1,2,0:T(8,128)(2,1)}), bf16[8,128,256]{1,2,0:T(8,128)(2,1)S(1)}, u32[]{:S(2)}, u32[]{:S(2)}) async-start(bf16[8,128,256]{1,2,0:T(8,128)(2,1)} %copy.110), calls=%async_computation.8 | async-start | bytes 1048576 | tf_op jit(solution)/shard_map/all_to_all | solution.py:119
  155.9 8.1 %all-to-all-done.8 = bf16[8,128,256]{1,2,0:T(8,128)(2,1)S(1)} async-done(((bf16[8,128,256]{1,2,0:T(8,128)(2,1)}), bf16[8,128,256]{1,2,0:T(8,128)(2,1)S(1)}, u32[]{:S(2)}, u32[]{:S(2)}) %all-to-all-start.8) | async-done | bytes 524320 | tf_op jit(solution)/shard_map/all_to_all | solution.py:119
  164.1 3.5 %all-to-all-start.7 = ((bf16[8,128,256]{1,2,0:T(8,128)(2,1)}), bf16[8,128,256]{1,2,0:T(8,128)(2,1)S(1)}, u32[]{:S(2)}, u32[]{:S(2)}) async-start(bf16[8,128,256]{1,2,0:T(8,128)(2,1)} %copy.108), calls=%async_computation.7 | async-start | bytes 1048576 | tf_op jit(solution)/shard_map/all_to_all | solution.py:118
  167.6 1.3 copy.102
  168.9 1.0 copy.111
  169.9 1.0 copy.113
  170.9 5.1 %all-to-all-done.7 = bf16[8,128,256]{1,2,0:T(8,128)(2,1)S(1)} async-done(((bf16[8,128,256]{1,2,0:T(8,128)(2,1)}), bf16[8,128,256]{1,2,0:T(8,128)(2,1)S(1)}, u32[]{:S(2)}, u32[]{:S(2)}) %all-to-all-start.7) | async-done | bytes 524320 | tf_op jit(solution)/shard_map/all_to_all | solution.py:118
  176.0 1.0 copy.112
  (50 shorter events, 11.1 us)
Async XLA Ops:
  0.6 26.3 %copy-start.5 = (bf16[128,2048]{1,0:T(8,128)(2,1)S(1)}, bf16[128,2048]{1,0:T(8,128)(2,1)}, u32[]{:S(2)}) copy-start(bf16[128,2048]{1,0:T(8,128)(2,1)} %param.17) | copy-start | bytes 1572868
  0.6 11.8 %all-to-all-start.3 = ((f32[128,8,2]{0,2,1:T(2,128)}), f32[128,8,2]{0,2,1:T(2,128)S(1)}, u32[]{:S(2)}, u32[]{:S(2)}) async-start(f32[128,8,2]{0,2,1:T(2,128)} %bitcast.93), calls=%async_computation.3 | async-start | bytes 16384 | tf_op jit(solution)/shard_map/all_to_all | solution.py:79
  7.4 30.5 %copy-start.6 = (bf16[128,2048]{1,0:T(8,128)(2,1)S(1)}, bf16[128,2048]{1,0:T(8,128)(2,1)}, u32[]{:S(2)}) copy-start(bf16[128,2048]{1,0:T(8,128)(2,1)} %param.18) | copy-start | bytes 1572868
  12.5 11.0 %all-to-all-start = ((bf16[128,8,256]{0,2,1:T(8,128)(2,1)}), bf16[128,8,256]{0,2,1:T(8,128)(2,1)S(1)}, u32[]{:S(2)}, u32[]{:S(2)}) async-start(bf16[128,8,256]{0,2,1:T(8,128)(2,1)} %bitcast), calls=%async_computation | async-start | bytes 1048576 | tf_op jit(solution)/shard_map/all_to_all | solution.py:74
  16.0 33.7 %copy-start.7 = (bf16[128,2048]{1,0:T(8,128)(2,1)S(1)}, bf16[128,2048]{1,0:T(8,128)(2,1)}, u32[]{:S(2)}) copy-start(bf16[128,2048]{1,0:T(8,128)(2,1)} %param.14) | copy-start | bytes 1572868
  23.5 11.0 %all-to-all-start.1 = ((bf16[128,8,256]{0,2,1:T(8,128)(2,1)}), bf16[128,8,256]{0,2,1:T(8,128)(2,1)S(1)}, u32[]{:S(2)}, u32[]{:S(2)}) async-start(bf16[128,8,256]{0,2,1:T(8,128)(2,1)} %bitcast.2), calls=%async_computation.1 | async-start | bytes 1048576 | tf_op jit(solution)/shard_map/all_to_all | solution.py:75
  34.4 11.0 %all-to-all-start.5 = ((bf16[128,8,256]{2,0,1:T(8,128)(2,1)}), bf16[128,8,256]{2,0,1:T(8,128)(2,1)S(1)}, u32[]{:S(2)}, u32[]{:S(2)}) async-start(bf16[128,8,256]{2,0,1:T(8,128)(2,1)} %bitcast.72), calls=%async_computation.5 | async-start | bytes 1048576 | tf_op jit(solution)/shard_map/all_to_all | solution.py:76
  45.4 0.8 copy-start.4
  46.2 11.0 %all-to-all-start.4 = ((bf16[128,8,256]{2,0,1:T(8,128)(2,1)}), bf16[128,8,256]{2,0,1:T(8,128)(2,1)S(1)}, u32[]{:S(2)}, u32[]{:S(2)}) async-start(bf16[128,8,256]{2,0,1:T(8,128)(2,1)} %bitcast.73), calls=%async_computation.4 | async-start | bytes 1048576 | tf_op jit(solution)/shard_map/all_to_all | solution.py:77
  57.2 19.0 %all-to-all-start.2 = ((bf16[128,8,256]{2,0,1:T(8,128)(2,1)}), bf16[128,8,256]{2,0,1:T(8,128)(2,1)S(1)}, u32[]{:S(2)}, u32[]{:S(2)}) async-start(bf16[128,8,256]{2,0,1:T(8,128)(2,1)} %bitcast.74), calls=%async_computation.2 | async-start | bytes 1048576 | tf_op jit(solution)/shard_map/all_to_all | solution.py:73
  61.6 37.5 %copy-start = (bf16[1024,2,128]{2,0,1:T(8,128)(2,1)}, bf16[1024,2,128]{2,0,1:T(8,128)(2,1)S(1)}, u32[]{:S(2)}) copy-start(bf16[1024,2,128]{2,0,1:T(8,128)(2,1)S(1)} %copy.89) | copy-start | bytes 1572868
  62.4 36.6 %copy-start.2 = (bf16[1024,2,128]{2,0,1:T(8,128)(2,1)}, bf16[1024,2,128]{2,0,1:T(8,128)(2,1)S(1)}, u32[]{:S(2)}) copy-start(bf16[1024,2,128]{2,0,1:T(8,128)(2,1)S(1)} %copy.90) | copy-start | bytes 1572868
  63.6 26.7 %collective-permute-start.1 = (bf16[512,4,128]{2,0,1:T(8,128)(2,1)}, bf16[512,4,128]{2,0,1:T(8,128)(2,1)}, u32[]{:S(2)}, u32[]{:S(2)}) collective-permute-start(bf16[512,4,128]{2,0,1:T(8,128)(2,1)} %get-tuple-element.63), channel_id=1, source_target_pairs={{1,0},{2,1},{3,2},{4,3},{5,4},{6,5},{7,6},{8,7},{9,8},{10,9},{11,1... | collective-permute-start | bytes 1572872 | tf_op jit(solution)/shard_map/ppermute | solution.py:20
  82.4 14.5 %collective-permute-start = (bf16[512,4,128]{2,0,1:T(8,128)(2,1)}, bf16[512,4,128]{2,0,1:T(8,128)(2,1)S(1)}, u32[]{:S(2)}, u32[]{:S(2)}) collective-permute-start(bf16[512,4,128]{2,0,1:T(8,128)(2,1)} %get-tuple-element.62), channel_id=1, source_target_pairs={{0,1},{1,2},{2,3},{3,4},{4,5},{5,6},{6,7},{7,8},{8,9},{9,10},{10,1... | collective-permute-start | bytes 1572872 | tf_op jit(solution)/shard_map/ppermute | solution.py:18
  102.2 14.6 %copy-start.1 = (bf16[1024,2,128]{2,0,1:T(8,128)(2,1)S(1)}, bf16[1024,2,128]{2,0,1:T(8,128)(2,1)}, u32[]{:S(2)}) copy-start(bf16[1024,2,128]{2,0,1:T(8,128)(2,1)} %copy-done) | copy-start | bytes 1572868
  102.2 14.6 %copy-start.3 = (bf16[1024,2,128]{2,0,1:T(8,128)(2,1)S(1)}, bf16[1024,2,128]{2,0,1:T(8,128)(2,1)}, u32[]{:S(2)}) copy-start(bf16[1024,2,128]{2,0,1:T(8,128)(2,1)} %copy-done.2) | copy-start | bytes 1572868
  103.2 23.7 %collective-permute-start.2 = (f32[512,4,128]{2,0,1:T(8,128)}, f32[512,4,128]{2,0,1:T(8,128)}, u32[]{:S(2)}, u32[]{:S(2)}) collective-permute-start(f32[512,4,128]{2,0,1:T(8,128)} %slice.218), channel_id=1, source_target_pairs={{0,1},{1,2},{2,3},{3,4},{4,5},{5,6},{6,7},{7,8},{8,9},{9,10},{10,1... | collective-permute-start | bytes 3145736 | tf_op jit(solution)/shard_map/ppermute | solution.py:29
  108.6 35.2 %collective-permute-start.3 = (f32[512,4,128]{2,0,1:T(8,128)}, f32[512,4,128]{2,0,1:T(8,128)}, u32[]{:S(2)}, u32[]{:S(2)}) collective-permute-start(f32[512,4,128]{2,0,1:T(8,128)} %fusion.21), channel_id=1, source_target_pairs={{0,63},{1,0},{2,1},{3,2},{4,3},{5,4},{6,5},{7,6},{8,7},{9,8},{10,9... | collective-permute-start | bytes 3145736 | tf_op jit(solution)/shard_map/ppermute | solution.py:29
  122.2 29.0 %all-to-all-start.6 = ((bf16[8,128,256]{2,1,0:T(8,128)(2,1)}), bf16[8,128,256]{2,1,0:T(8,128)(2,1)}, u32[]{:S(2)}, u32[]{:S(2)}) async-start(bf16[8,128,256]{2,1,0:T(8,128)(2,1)} %bitcast.79), calls=%async_computation.6 | async-start | bytes 1048576 | tf_op jit(solution)/shard_map/all_to_all | solution.py:117
  151.2 12.8 %all-to-all-start.8 = ((bf16[8,128,256]{1,2,0:T(8,128)(2,1)}), bf16[8,128,256]{1,2,0:T(8,128)(2,1)S(1)}, u32[]{:S(2)}, u32[]{:S(2)}) async-start(bf16[8,128,256]{1,2,0:T(8,128)(2,1)} %copy.110), calls=%async_computation.8 | async-start | bytes 1048576 | tf_op jit(solution)/shard_map/all_to_all | solution.py:119
  164.1 11.9 %all-to-all-start.7 = ((bf16[8,128,256]{1,2,0:T(8,128)(2,1)}), bf16[8,128,256]{1,2,0:T(8,128)(2,1)S(1)}, u32[]{:S(2)}, u32[]{:S(2)}) async-start(bf16[8,128,256]{1,2,0:T(8,128)(2,1)} %copy.108), calls=%async_computation.7 | async-start | bytes 1048576 | tf_op jit(solution)/shard_map/all_to_all | solution.py:118
where the time goes:
time: 180 us; the launch traced here: 177 us
  starting transfers between devices  65.7 us (36%)
  waiting for transfers between devices  63.4 us (35%)
  local copies, waits for them, and re-layouts  22.9 us (13%)
  matrix products  13.9 us (8%)
  other arithmetic  9.99 us (6%)
    ppermute x2, waiting for transfers between devices, from_behind(): lax.ppermute(shard, axis, [(i, (i + by) % length) for i in range(length)])  15.5 us
    ppermute x2, starting transfers between devices, from_behind(): lax.ppermute(shard, axis, [(i, (i + by) % length) for i in range(length)])  12.5 us
    ppermute x1, starting transfers between devices, padded(): lax.ppermute(head, axis, [((i + 1) % count, i) for i in range(count)])  11.4 us
    unnamed x25, local copies, waits for them, and re-layouts  8.46 us
    all_to_all x1, waiting for transfers between devices, per_device(): lax.all_to_all(merge_heads(value_total), 'head', split_axis=0, concat_axi...  8.14 us
    all_to_all x1, starting transfers between devices, per_device(): lax.all_to_all(log_sum, 'head', split_axis=1, concat_axis=0, tiled=True)  6.8 us
    all_to_all x1, waiting for transfers between devices, per_device(): lax.all_to_all(values, 'head', split_axis=1, concat_axis=0, tiled=True)  6.64 us
    all_to_all x1, waiting for transfers between devices, per_device(): lax.all_to_all(outputs, 'head', split_axis=1, concat_axis=0, tiled=True)  6.64 us
  transfers between devices with their start and end apart: 13, of which 10 were waited for; matrix products, arithmetic and copies ran while one was open for 22% of the time, Pallas kernels for 0%

commit v1 on v0

v1 whole, which is shorter than its diff:
```python
import math

import jax
import jax.numpy as jnp
from jax import lax
from jax.experimental import pallas as pl
from jax.experimental.pallas import tpu as pltpu
from jax.sharding import PartitionSpec as P

MESH = pl.DeviceIdType.MESH
HD = 128
SCALE = HD**-0.5
LOG2E = math.log2(math.e)
F32 = jnp.float32
BF16 = jnp.bfloat16
NX = 4
SLOTS = 2 * NX
BLOCKS = 4
ROWS = SLOTS * 128
HALF = 256


def nt(a, b, **kw):
    return lax.dot_general(a, b, (((1,), (1,)), ((), ())), preferred_element_type=F32, **kw)


def nn(a, b, **kw):
    return lax.dot_general(a, b, (((1,), (0,)), ((), ())), preferred_element_type=F32, **kw)


def tn(a, b):
    return lax.dot_general(a, b, (((0,), (0,)), ((), ())), preferred_element_type=F32)


def tile(k, v, q, g, lse, delta):
    p = jnp.exp2(nt(k, q) * (SCALE * LOG2E) - lse)
    ds = (p * (nt(v, g) - delta)).astype(BF16)
    dv = nn(p.astype(BF16), g)
    dk = nn(ds, q)
    dq = tn(ds, k)
    return dk, dv, dq


def kernel(
    groups,
    q_in, k_in, v_in, o_in, g_in, l_in,
    dq_res, dk_res, dv_res,
    qg, kv, kvp, eqg, st_all, st, est, g_v, o_v, l_v,
    dq_acc, dq_own, dk_acc, dv_acc,
    dq_oth, dq_got, dq_out, dk_out, dv_out, dqe_out, dqe_got, dkv_out, dkv_got,
    loc, r_qg, r_kv, r_b, r_k, r_c, r_st, r_dqe, r_dkv, r_d, r_out,
    s_a, s_b, s_k, s_c, s_st, s_st2, s_dqe, s_dkv, s_d, s_out,
):
    head = lax.axis_index("head")
    blk = lax.axis_index("blk")
    x = lax.div(head, 2)
    zl = lax.rem(head, 2)
    grp = lax.div(blk, 2)
    c = lax.rem(blk, 2)
    me_t = x * 2 + c
    me_s = c * NX + x
    my_b = lax.div(me_s, 2)
    eb = 3 * zl
    pb = 3 - eb
    partner = (x * 2 + (1 - zl), blk)
    near = (x * 2 + (1 - zl), lax.rem(grp + 2 * zl - 1 + groups, groups) * 2 + c)

    def at_t(t):
        return (lax.div(t, 2) * 2 + zl, grp * 2 + lax.rem(t, 2))

    def at_s(s):
        return (lax.rem(s, NX) * 2 + zl, grp * 2 + lax.div(s, NX))

    def rows(b):
        return pl.ds(pl.multiple_of(b * HALF, HALF), HALF)

    def run(s):
        return pl.ds(pl.multiple_of(s * 128, 128), 128)

    def cols(t, hl):
        return pl.ds(pl.multiple_of(t * 256 + hl * 128, 128), 128)

    def remote(src, dst, ssem, rsem, device):
        copy = pltpu.make_async_remote_copy(
            src_ref=src, dst_ref=dst, send_sem=ssem, recv_sem=rsem, device_id=device, device_id_type=MESH
        )
        copy.start()
        return copy

    def arrived(ref, sem):
        pltpu.make_async_copy(ref, ref, sem).wait()

    pending = []

    locals_ = [
        pltpu.make_async_copy(g_in, g_v, loc.at[0]),
        pltpu.make_async_copy(o_in, o_v, loc.at[1]),
        pltpu.make_async_copy(l_in, l_v, loc.at[2]),
    ]
    for copy in locals_:
        copy.start()

    barrier = pltpu.get_barrier_semaphore()
    for o in range(1, SLOTS):
        pl.semaphore_signal(
            barrier, inc=1, device_id=at_t(lax.rem(me_t + o, SLOTS)), device_id_type=MESH
        )
    for device in (partner, near):
        pl.semaphore_signal(barrier, inc=1, device_id=device, device_id_type=MESH)
    pl.semaphore_wait(barrier, SLOTS + 1)

    def spread(hl, which):
        arrays = ((q_in, qg.at[0, 0, hl], 0), (g_in, qg.at[0, 1, hl], 1)) if which == 0 else (
            (k_in, kv.at[0, hl], 2), (v_in, kv.at[1, hl], 3))
        rsem = r_qg.at[hl, my_b] if which == 0 else r_kv.at[hl]
        for src, dst, _ in arrays:
            pltpu.make_async_copy(src.at[:, cols(me_t, hl)], dst.at[run(me_s)], rsem).start()
        for o in range(1, SLOTS):
            t = lax.rem(me_t + o, SLOTS)
            for src, dst, n in arrays:
                remote(src.at[:, cols(t, hl)], dst.at[run(me_s)], s_a.at[n, hl], rsem, at_t(t))

    spread(0, 0)
    spread(0, 1)

    for copy in locals_:
        copy.wait()
    r = lax.broadcasted_iota(jnp.int32, (8 * SLOTS, SLOTS * 256), 0)
    col = lax.broadcasted_iota(jnp.int32, (8 * SLOTS, SLOTS * 256), 1)
    wanted = lax.shift_right_logical(r, 3) * 2 + lax.shift_right_logical(r & 7, 1)
    pick = jnp.where(
        (lax.shift_right_logical(col, 7) == wanted) & ((r & 1) == 1) & ((r & 7) < 4), 1.0, 0.0
    ).astype(F32)
    prod = g_v[...].astype(F32) * o_v[...].astype(F32)
    delta_rows = nt(pick, prod, precision=lax.Precision.HIGHEST)
    r2 = lax.broadcasted_iota(jnp.int32, (8 * SLOTS, 2 * SLOTS), 0)
    col2 = lax.broadcasted_iota(jnp.int32, (8 * SLOTS, 2 * SLOTS), 1)
    wanted2 = lax.shift_right_logical(r2, 3) * 2 + lax.shift_right_logical(r2 & 7, 1)
    pick2 = jnp.where((col2 == wanted2) & ((r2 & 1) == 0) & ((r2 & 7) < 4), 1.0, 0.0).astype(F32)
    lse_rows = nn(pick2, l_v[...], precision=lax.Precision.HIGHEST) * LOG2E
    st_all[...] = delta_rows + lse_rows
    mine = st_all.at[pl.ds(pl.multiple_of(me_t * 8, 8), 8)]
    pltpu.make_async_copy(mine, st.at[0, me_s], r_st.at[0]).start()
    for o in range(1, SLOTS):
        t = lax.rem(me_t + o, SLOTS)
        pending.append(remote(
            st_all.at[pl.ds(pl.multiple_of(t * 8, 8), 8)], st.at[0, me_s], s_st.at[o], r_st.at[0], at_t(t)
        ))

    dk_acc[...] = jnp.zeros_like(dk_acc)
    dv_acc[...] = jnp.zeros_like(dv_acc)

    order = [pb + i * (1 - 2 * lax.div(pb, 3)) for i in range(BLOCKS)]

    def forward(hl):
        for b in order:
            arrived(qg.at[0, :, hl, rows(b)], r_qg.at[hl, b])
            pending.append(remote(
                qg.at[0, :, hl, rows(b)], qg.at[1, :, hl, rows(b)], s_b.at[hl, b], r_b.at[hl, b], partner
            ))
        pending.append(remote(
            qg.at[0, :, hl, rows(eb)], eqg.at[hl, :, pl.ds(0, HALF)], s_c.at[hl, 0], r_c.at[hl], near
        ))

    def forward_kv(hl):
        arrived(kv.at[:, hl], r_kv.at[hl])
        pending.append(remote(kv.at[:, hl, rows(pb)], kvp.at[hl], s_k.at[hl], r_k.at[hl], partner))

    def forward_edge(hl):
        arrived(qg.at[1, :, hl, rows(eb)], r_b.at[hl, eb])
        pending.append(remote(
            qg.at[1, :, hl, rows(eb)], eqg.at[hl, :, pl.ds(HALF, HALF)], s_c.at[hl, 1], r_c.at[hl], near
        ))

    forward(0)
    spread(1, 0)
    arrived(st.at[0], r_st.at[0])
    pending.append(remote(st.at[0], st.at[1], s_st2.at[0], r_st.at[1], partner))
    forward_kv(0)
    spread(1, 1)
    arrived(st.at[1], r_st.at[1])
    pending.append(remote(st.at[:, pl.ds(2 * eb, 2)], est, s_st2.at[1], r_st.at[2], near))
    forward_edge(0)
    forward(1)
    arrived(est, r_st.at[2])

    def stat(ref, first, hl, n):
        place = 2 * hl + n
        return jnp.concatenate(
            [ref[p, first + j, place : place + 1, :] for p in range(2) for j in range(2)], axis=1
        )

    def edge(hl):
        arrived(kvp.at[hl], r_k.at[hl])
        arrived(eqg.at[hl], r_c.at[hl])
        q = eqg[hl, 0]
        g = eqg[hl, 1]
        lse = stat(est, 0, hl, 0)
        delta = stat(est, 0, hl, 1)
        dk, dv, dq = tile(kvp[hl, 0], kvp[hl, 1], q, g, lse, delta)
        dkv_out[hl, 0] = (dk * SCALE).astype(BF16)
        dkv_out[hl, 1] = dv.astype(BF16)
        pending.append(remote(dkv_out.at[hl], dkv_got.at[hl], s_dkv.at[hl], r_dkv.at[hl], partner))
        dk, dv, dq2 = tile(kv[0, hl, rows(eb)], kv[1, hl, rows(eb)], q, g, lse, delta)
        dqe_out[hl] = ((dq + dq2) * SCALE).astype(BF16)
        pending.append(remote(dqe_out.at[hl], dqe_got.at[hl], s_dqe.at[hl], r_dqe.at[hl], near))
        dk_acc[hl, rows(eb)] += dk
        dv_acc[hl, rows(eb)] += dv

    def give_back(buf, res, n, hl, b):
        for j in range(2):
            s = 2 * b + j
            src = buf.at[hl, run(s)]
            dst = res.at[:, cols(me_t, hl)]

            @pl.when(s == me_s)
            def _():
                pltpu.make_async_copy(src, dst, r_out.at[n]).start()

            @pl.when(s != me_s)
            def _():
                remote(src, dst, s_out.at[n], r_out.at[n], at_s(s))

    def finish_keys(hl, b, first):
        dk = dk_acc[hl, rows(b)] * SCALE
        dv = dv_acc[hl, rows(b)]
        if first:
            arrived(dkv_got.at[hl], r_dkv.at[hl])
            dk = dk + dkv_got[hl, 0].astype(F32)
            dv = dv + dkv_got[hl, 1].astype(F32)
        dk_out[hl, rows(b)] = dk.astype(BF16)
        dv_out[hl, rows(b)] = dv.astype(BF16)
        give_back(dk_out, dk_res, 1, hl, b)
        give_back(dv_out, dv_res, 2, hl, b)

    def finish_queries(hl, b):
        arrived(dq_got.at[hl, rows(b)], r_d.at[hl, b])
        dq_out[hl, rows(b)] = (dq_own[hl, rows(b)] + dq_got[hl, rows(b)].astype(F32)).astype(BF16)
        give_back(dq_out, dq_res, 0, hl, b)

    def main(hl, i):
        b = order[i]
        if i < BLOCKS - 1:
            arrived(qg.at[1, :, hl, rows(b)], r_b.at[hl, b])
        q = jnp.concatenate([qg[0, 0, hl, rows(b)], qg[1, 0, hl, rows(b)]], axis=0)
        g = jnp.concatenate([qg[0, 1, hl, rows(b)], qg[1, 1, hl, rows(b)]], axis=0)
        lse = stat(st, 2 * b, hl, 0)
        delta = stat(st, 2 * b, hl, 1)
        dq_acc[...] = jnp.zeros_like(dq_acc)

        def body(kb, carry):
            dk, dv, dq = tile(kv[0, hl, rows(kb)], kv[1, hl, rows(kb)], q, g, lse, delta)
            dk_acc[hl, rows(kb)] += dk
            dv_acc[hl, rows(kb)] += dv
            dq_acc[...] += dq
            return carry

        lax.fori_loop(jnp.maximum(b - 1, 0), jnp.minimum(b + 1, BLOCKS - 1) + 1, body, 0)
        own = dq_acc[pl.ds(0, HALF)] * SCALE
        other = dq_acc[pl.ds(HALF, HALF)] * SCALE
        if i == BLOCKS - 1:
            arrived(dqe_got.at[hl], r_dqe.at[hl])
            own = own + dqe_got[hl, pl.ds(0, HALF)].astype(F32)
            other = other + dqe_got[hl, pl.ds(HALF, HALF)].astype(F32)
        dq_oth[hl, rows(b)] = other.astype(BF16)
        pending.append(remote(
            dq_oth.at[hl, rows(b)], dq_got.at[hl, rows(b)], s_d.at[hl, b], r_d.at[hl, b], partner
        ))
        dq_own[hl, rows(b)] = own
        if i >= 1:
            finish_keys(hl, order[i - 1], i == 1)

    edge(0)
    forward_kv(1)
    forward_edge(1)
    for i in range(BLOCKS):
        main(0, i)
    finish_keys(0, order[BLOCKS - 1], False)
    edge(1)
    for i in reversed(range(BLOCKS)):
        finish_queries(0, order[i])
    for i in range(BLOCKS - 1):
        main(1, i)
    finish_queries(1, order[2])
    main(1, BLOCKS - 1)
    finish_keys(1, order[BLOCKS - 1], False)
    for i in (1, 3, 0):
        finish_queries(1, order[i])

    for copy in pending:
        copy.wait_send()
    for n in range(4):
        for hl in range(2):
            arrived(kv.at[0, 0, pl.ds(0, 7 * 128)], s_a.at[n, hl])
    for n, res in enumerate((dq_res, dk_res, dv_res)):
        arrived(dk_out.at[:, pl.ds(0, 7 * 128)], s_out.at[n])
        arrived(res, r_out.at[n])


def per_device(queries, keys, values, outputs, out_grad, log_sum):
    groups = lax.axis_size("blk") // 2
    tokens, width = queries.shape
    any_ = pl.BlockSpec(memory_space=pl.ANY)
    dma = pltpu.SemaphoreType.DMA
    result = jax.ShapeDtypeStruct((tokens, width), BF16)
    scratch = [
        pltpu.VMEM((2, 2, 2, ROWS, HD), BF16),
        pltpu.VMEM((2, 2, ROWS, HD), BF16),
        pltpu.VMEM((2, 2, HALF, HD), BF16),
        pltpu.VMEM((2, 2, 2 * HALF, HD), BF16),
        pltpu.VMEM((8 * SLOTS, 128), F32),
        pltpu.VMEM((2, SLOTS, 8, 128), F32),
        pltpu.VMEM((2, 2, 8, 128), F32),
        pltpu.VMEM((tokens, width), BF16),
        pltpu.VMEM((tokens, width), BF16),
        pltpu.VMEM(log_sum.shape[::-1], F32),
        pltpu.VMEM((2 * HALF, HD), F32),
        pltpu.VMEM((2, ROWS, HD), F32),
        pltpu.VMEM((2, ROWS, HD), F32),
        pltpu.VMEM((2, ROWS, HD), F32),
        pltpu.VMEM((2, ROWS, HD), BF16),
        pltpu.VMEM((2, ROWS, HD), BF16),
        pltpu.VMEM((2, ROWS, HD), BF16),
        pltpu.VMEM((2, ROWS, HD), BF16),
        pltpu.VMEM((2, ROWS, HD), BF16),
        pltpu.VMEM((2, 2 * HALF, HD), BF16),
        pltpu.VMEM((2, 2 * HALF, HD), BF16),
        pltpu.VMEM((2, 2, HALF, HD), BF16),
        pltpu.VMEM((2, 2, HALF, HD), BF16),
        dma((3,)),
        dma((2, BLOCKS)),
        dma((2,)),
        dma((2, BLOCKS)),
        dma((2,)),
        dma((2,)),
        dma((3,)),
        dma((2,)),
        dma((2,)),
        dma((2, BLOCKS)),
        dma((3,)),
        dma((4, 2)),
        dma((2, BLOCKS)),
        dma((2,)),
        dma((2, 2)),
        dma((SLOTS,)),
        dma((2,)),
        dma((2,)),
        dma((2,)),
        dma((2, BLOCKS)),
        dma((3,)),
    ]

    def body(*refs):
        kernel(groups, *refs)

    return pl.pallas_call(
        body,
        out_shape=(result, result, result),
        in_specs=[any_] * 6,
        out_specs=(any_, any_, any_),
        scratch_shapes=scratch,
        compiler_params=pltpu.CompilerParams(
            collective_id=0, has_side_effects=True, vmem_limit_bytes=60 * 2**20
        ),
        cost_estimate=pl.CostEstimate(flops=4 * 10**9, bytes_accessed=4 * 2**20, transcendentals=3 * 2**20),
        name="attention_backward",
    )(queries, keys, values, outputs, out_grad, jnp.transpose(log_sum))


def solution(mesh):
    spec = P(("blk", "head"), None)
    return jax.shard_map(
        per_device, mesh=mesh, in_specs=(spec,) * 6, out_specs=(spec,) * 3, check_vma=False
    )
```

time: 180 us -> 79.7 us (0.44); the launches traced: 177 us -> 79.5 us
  Pallas kernels: 0 us -> 74.8 us
  starting transfers between devices: 65.7 us -> 0 us
  waiting for transfers between devices: 63.4 us -> 0 us
  local copies, waits for them, and re-layouts: 22.9 us -> 3.97 us
  matrix products: 13.9 us -> 0 us
  other arithmetic: 9.99 us -> 0 us
    pallas_call x0 -> x1, Pallas kernels: none -> 74.8 us  [per_device(): pl.pallas_call(body, out_shape=(result, result, result), in_specs=[any_]...]
    all_to_all x9 -> x0, waiting for transfers between devices: 45.9 us -> none  [the longest x1 8.14 us: per_device(): lax.all_to_all(merge_heads(value_total), 'head', split_axis=0, concat_axi...]
    all_to_all x9 -> x0, starting transfers between devices: 35.9 us -> none  [the longest x1 6.8 us: per_device(): lax.all_to_all(log_sum, 'head', split_axis=1, concat_axis=0, tiled=True)]
    ppermute x4 -> x0, starting transfers between devices: 29.8 us -> none  [the longest x2 12.5 us: from_behind(): lax.ppermute(shard, axis, [(i, (i + by) % length) for i in range(length)])]
    ppermute x4 -> x0, waiting for transfers between devices: 17.4 us -> none  [the longest x2 15.5 us: from_behind(): lax.ppermute(shard, axis, [(i, (i + by) % length) for i in range(length)])]
    dot_general x10 -> x0, matrix products: 13.9 us -> none  [the longest x2 4.22 us: block_terms(): jnp.einsum('qhd,khd->hqk', grad_rows, value_rows, preferred_element_type=...]
    all_to_all x8 -> x0, local copies, waits for them, and re-layouts: 6.24 us -> none  [the longest x1 1.31 us: per_device(): lax.all_to_all(merge_heads(query_total), 'head', split_axis=0, concat_axi...]
    unnamed x25 -> x7, local copies, waits for them, and re-layouts: 8.46 us -> 3.97 us
  transfers between devices with their start and end apart: 13 -> 0, of which waited for: 10 -> 0; matrix products, arithmetic and copies ran while one was open for 22% -> 0% of each run, Pallas kernels for 0% -> 0%
where the time goes in v1:
time: 79.7 us; the launch traced here: 79.5 us
  Pallas kernels  74.8 us (94%)
  local copies, waits for them, and re-layouts  3.97 us (5%)
    pallas_call x1, Pallas kernels, per_device(): pl.pallas_call(body, out_shape=(result, result, result), in_specs=[any_]...  74.8 us
    unnamed x7, local copies, waits for them, and re-layouts  3.97 us

profile of v1, /device:TPU:1, one launch (start us, length us, event | category | flops | bytes accessed | tf_op | source)
XLA Modules:
  0.0 79.5 jit_solution(3021904891056946062)
XLA Ops:
  0.6 74.8 %attention_backward.1 = (bf16[128,2048]{1,0:T(8,128)(2,1)}, bf16[128,2048]{1,0:T(8,128)(2,1)}, bf16[128,2048]{1,0:T(8,128)(2,1)}) custom-call(bf16[128,2048]{1,0:T(8,128)(2,1)} %refs_0_.1, bf16[128,2048]{1,0:T(8,128)(2,1)} %refs_1_.1, bf16[128,2048]{1,0:T(8,128)(2,1)} %refs_2_.1, bf16[128,2048]{1,0:T(8,128)(2,1)} %refs_3_.1, bf16[128,2048]{1,0:T(8,128)(2,1)} %refs_4_.1, ...), custom_call_target="tpu_custom_call" | custom-call | flops 4000000000 | bytes 4194304 | tf_op jit(solution)/shard_map/attention_backward/pallas_call | solution.py:356
  75.5 0.0 copy-start.1
  75.5 1.9 %copy.12 = bf16[128,2048]{1,0:T(8,128)(2,1)} copy(bf16[128,2048]{1,0:T(8,128)(2,1)} %get-tuple-element.6) | data formatting | bytes 1048576
  77.4 0.0 copy-done.1
  77.4 0.0 copy-start
  77.4 0.8 copy.13
  78.2 0.4 copy-done
  78.7 0.8 copy.14
Async XLA Ops:
  75.5 2.0 %copy-start.1 = (bf16[128,2048]{1,0:T(8,128)(2,1)S(1)}, bf16[128,2048]{1,0:T(8,128)(2,1)}, u32[]{:S(2)}) copy-start(bf16[128,2048]{1,0:T(8,128)(2,1)} %get-tuple-element.7) | copy-start | bytes 1572868
  77.4 1.2 %copy-start = (bf16[128,2048]{1,0:T(8,128)(2,1)S(1)}, bf16[128,2048]{1,0:T(8,128)(2,1)}, u32[]{:S(2)}) copy-start(bf16[128,2048]{1,0:T(8,128)(2,1)} %get-tuple-element.8) | copy-start | bytes 1572868

commit v2 on v1

v2 whole, which is shorter than its diff:
```python
import math

import jax
import jax.numpy as jnp
from jax import lax
from jax.experimental import pallas as pl
from jax.experimental.pallas import tpu as pltpu
from jax.sharding import PartitionSpec as P

MESH = pl.DeviceIdType.MESH
HD = 128
SCALE = HD**-0.5
LOG2E = math.log2(math.e)
F32 = jnp.float32
BF16 = jnp.bfloat16
NX = 4
SLOTS = 2 * NX
BLOCKS = 4
ROWS = SLOTS * 128
HALF = 256


def nt(a, b, **kw):
    return lax.dot_general(a, b, (((1,), (1,)), ((), ())), preferred_element_type=F32, **kw)


def nn(a, b, **kw):
    return lax.dot_general(a, b, (((1,), (0,)), ((), ())), preferred_element_type=F32, **kw)


def tn(a, b):
    return lax.dot_general(a, b, (((0,), (0,)), ((), ())), preferred_element_type=F32)


def tile(k, v, q, g, lse, delta):
    p = jnp.exp2(nt(k, q) * (SCALE * LOG2E) - lse)
    ds = (p * (nt(v, g) - delta)).astype(BF16)
    dv = nn(p.astype(BF16), g)
    dk = nn(ds, q)
    dq = tn(ds, k)
    return dk, dv, dq


def kernel(
    groups,
    q_in, k_in, v_in, o_in, g_in, l_in,
    dq_res, dk_res, dv_res,
    qg, kv, kvp, eqg, st_all, st, est, g_v, o_v, l_v,
    dq_edge, dq_own, dk_acc, dv_acc,
    dq_oth, dq_got, dq_out, dk_out, dv_out, dqe_out, dqe_got, dkv_out, dkv_got,
    loc, r_qg, r_kv, r_b, r_k, r_c, r_st, r_dqe, r_dkv, r_d, r_out,
    s_a, s_b, s_k, s_c, s_st, s_st2, s_dqe, s_dkv, s_d, s_out,
):
    head = lax.axis_index("head")
    blk = lax.axis_index("blk")
    x = lax.div(head, 2)
    zl = lax.rem(head, 2)
    grp = lax.div(blk, 2)
    c = lax.rem(blk, 2)
    me_t = x * 2 + c
    me_s = c * NX + x
    eb = 3 * zl
    pb = 3 - eb
    partner = (x * 2 + (1 - zl), blk)
    near = (x * 2 + (1 - zl), lax.rem(grp + 2 * zl - 1 + groups, groups) * 2 + c)
    order = [pb + i * (2 * zl - 1) for i in range(BLOCKS)]
    twin = [(x, 1 - c)]
    others = [(lax.rem(x + dx, NX), cc) for dx in (1, 3, 2) for cc in range(2)]

    def device_at(xt, ct):
        return (xt * 2 + zl, grp * 2 + ct)

    def rows(b):
        return pl.ds(pl.multiple_of(b * HALF, HALF), HALF)

    def run(s):
        return pl.ds(pl.multiple_of(s * 128, 128), 128)

    def cols(t, hl):
        return pl.ds(pl.multiple_of(t * 256 + hl * 128, 128), 128)

    def remote(src, dst, ssem, rsem, device):
        copy = pltpu.make_async_remote_copy(
            src_ref=src, dst_ref=dst, send_sem=ssem, recv_sem=rsem, device_id=device, device_id_type=MESH
        )
        copy.start()
        return copy

    def arrived(ref, sem):
        pltpu.make_async_copy(ref, ref, sem).wait()

    pending = []

    def arrays(hl, which):
        if which == 0:
            sem = r_qg.at[hl, me_s]
            return ((q_in, qg.at[0, 0, hl], 0, sem), (g_in, qg.at[0, 1, hl], 1, sem))
        sem = r_kv.at[hl]
        return ((k_in, kv.at[0, hl], 2, sem), (v_in, kv.at[1, hl], 3, sem))

    for hl in range(2):
        for src, dst, _, sem in arrays(hl, 0):
            pltpu.make_async_copy(src.at[:, cols(me_t, hl)], dst.at[run(me_s)], sem).start()
    locals_ = [
        pltpu.make_async_copy(g_in, g_v, loc.at[0]),
        pltpu.make_async_copy(o_in, o_v, loc.at[1]),
        pltpu.make_async_copy(l_in, l_v, loc.at[2]),
    ]
    for copy in locals_:
        copy.start()
    for hl in range(2):
        for src, dst, _, sem in arrays(hl, 1):
            pltpu.make_async_copy(src.at[:, cols(me_t, hl)], dst.at[run(me_s)], sem).start()

    barrier = pltpu.get_barrier_semaphore()
    for device in [device_at(*t) for t in twin + others] + [partner, near]:
        pl.semaphore_signal(barrier, inc=1, device_id=device, device_id_type=MESH)
    pl.semaphore_wait(barrier, SLOTS + 1)

    def spread(hl, which, targets):
        for xt, ct in targets:
            for src, dst, n, sem in arrays(hl, which):
                remote(
                    src.at[:, cols(xt * 2 + ct, hl)], dst.at[run(me_s)], s_a.at[n, hl], sem, device_at(xt, ct)
                )

    def forward(hl, s):
        arrived(qg.at[0, :, hl, run(s)], r_qg.at[hl, s])
        pending.append(remote(
            qg.at[0, :, hl, run(s)], qg.at[1, :, hl, run(s)], s_b.at[hl, s], r_b.at[hl, lax.div(s, 2)], partner
        ))

    spread(0, 0, twin)
    spread(1, 0, twin)
    spread(0, 0, others)
    for hl in range(2):
        forward(hl, me_s)
    spread(1, 0, others)
    twin_s = (1 - c) * NX + x
    for hl in range(2):
        forward(hl, twin_s)

    for copy in locals_:
        copy.wait()
    col = lax.broadcasted_iota(jnp.int32, (SLOTS * 256, 128), 0)
    r = lax.broadcasted_iota(jnp.int32, (SLOTS * 256, 128), 1)
    wanted = lax.shift_right_logical(r, 3) * 2 + lax.shift_right_logical(r & 7, 1)
    pick = jnp.where(
        (lax.shift_right_logical(col, 7) == wanted) & ((r & 1) == 1) & ((r & 7) < 4), 1.0, 0.0
    ).astype(BF16)
    prod = g_v[...].astype(F32) * o_v[...].astype(F32)
    high = prod.astype(BF16)
    low = (prod - high.astype(F32)).astype(BF16)
    sums = nn(high, pick) + nn(low, pick)
    st_all[...] = jnp.transpose(sums)[: 8 * SLOTS]
    for h in range(2 * SLOTS):
        place = 8 * (h // 2) + 2 * (h % 2)
        st_all[place : place + 1, :] = l_v[h : h + 1, :] * LOG2E
    mine = st_all.at[pl.ds(pl.multiple_of(me_t * 8, 8), 8)]
    pltpu.make_async_copy(mine, st.at[0, me_s], r_st.at[0]).start()
    for n, (xt, ct) in enumerate(twin + others):
        pending.append(remote(
            st_all.at[pl.ds(pl.multiple_of((xt * 2 + ct) * 8, 8), 8)],
            st.at[0, me_s], s_st.at[n], r_st.at[0], device_at(xt, ct),
        ))

    rest = [cc * NX + lax.rem(x + dx, NX) for dx in (3, 1, 2) for cc in range(2)]
    for s in rest:
        forward(0, s)
    spread(0, 1, twin + others)
    spread(1, 1, twin + others)
    for s in rest[:4]:
        forward(1, s)
    arrived(st.at[0], r_st.at[0])
    pending.append(remote(st.at[0], st.at[1], s_st2.at[0], r_st.at[1], partner))
    for s in rest[4:]:
        forward(1, s)

    dk_acc[...] = jnp.zeros_like(dk_acc)
    dv_acc[...] = jnp.zeros_like(dv_acc)

    def forward_kv(hl):
        arrived(kv.at[:, hl], r_kv.at[hl])
        pending.append(remote(kv.at[:, hl, rows(pb)], kvp.at[hl], s_k.at[hl], r_k.at[hl], partner))

    def forward_edge(hl):
        pending.append(remote(
            qg.at[0, :, hl, rows(eb)], eqg.at[hl, :, pl.ds(0, HALF)], s_c.at[hl, 0], r_c.at[hl], near
        ))
        arrived(qg.at[1, :, hl, rows(eb)], r_b.at[hl, eb])
        pending.append(remote(
            qg.at[1, :, hl, rows(eb)], eqg.at[hl, :, pl.ds(HALF, HALF)], s_c.at[hl, 1], r_c.at[hl], near
        ))

    def stat(ref, parities, first, hl, n):
        place = 2 * hl + n
        return jnp.concatenate(
            [ref[p, first + j, place : place + 1, :] for p in parities for j in range(2)], axis=1
        )

    def queries(hl, parity, i):
        b = order[i]
        if parity == 1 and i < BLOCKS - 1:
            arrived(qg.at[1, :, hl, rows(b)], r_b.at[hl, b])
        count = (2 if i in (0, BLOCKS - 1) else 3) * HALF
        keys = pl.ds(pl.multiple_of(jnp.maximum(b - 1, 0) * HALF, HALF), count)
        dk, dv, dq = tile(
            kv[0, hl, keys], kv[1, hl, keys], qg[parity, 0, hl, rows(b)], qg[parity, 1, hl, rows(b)],
            stat(st, (parity,), 2 * b, hl, 0), stat(st, (parity,), 2 * b, hl, 1),
        )
        dk_acc[hl, keys] += dk
        dv_acc[hl, keys] += dv
        dq = dq * SCALE
        if parity == 0:
            dq_own[hl, rows(b)] = dq
        elif i == BLOCKS - 1:
            dq_edge[hl] = dq
        else:
            dq_oth[hl, rows(b)] = dq.astype(BF16)

    def edge(hl):
        arrived(kvp.at[hl], r_k.at[hl])
        arrived(eqg.at[hl], r_c.at[hl])
        dk, dv, dq = tile(
            jnp.concatenate([kvp[hl, 0], kv[0, hl, rows(eb)]], axis=0),
            jnp.concatenate([kvp[hl, 1], kv[1, hl, rows(eb)]], axis=0),
            eqg[hl, 0], eqg[hl, 1], stat(est, (0, 1), 0, hl, 0), stat(est, (0, 1), 0, hl, 1),
        )
        dqe_out[hl] = (dq * SCALE).astype(BF16)
        pending.append(remote(dqe_out.at[hl], dqe_got.at[hl], s_dqe.at[hl], r_dqe.at[hl], near))
        dkv_out[hl, 0] = (dk[:HALF] * SCALE).astype(BF16)
        dkv_out[hl, 1] = dv[:HALF].astype(BF16)
        dk_acc[hl, rows(eb)] += dk[HALF:]
        dv_acc[hl, rows(eb)] += dv[HALF:]

    def send_edge_keys(hl):
        pending.append(remote(dkv_out.at[hl], dkv_got.at[hl], s_dkv.at[hl], r_dkv.at[hl], partner))

    def send_queries(hl, i):
        b = order[i]
        if i == BLOCKS - 1:
            arrived(dqe_got.at[hl], r_dqe.at[hl])
            dq_oth[hl, rows(b)] = (dq_edge[hl] + dqe_got[hl, pl.ds(HALF, HALF)].astype(F32)).astype(BF16)
        pending.append(remote(
            dq_oth.at[hl, rows(b)], dq_got.at[hl, rows(b)], s_d.at[hl, b], r_d.at[hl, b], partner
        ))

    def give_back(buf, res, n, hl, b):
        for j in range(2):
            s = 2 * b + j
            src = buf.at[hl, run(s)]
            dst = res.at[:, cols(me_t, hl)]

            @pl.when(s == me_s)
            def _():
                pltpu.make_async_copy(src, dst, r_out.at[n]).start()

            @pl.when(s != me_s)
            def _():
                remote(src, dst, s_out.at[n], r_out.at[n], device_at(lax.rem(s, NX), lax.div(s, NX)))

    def finish_keys(hl, i):
        b = order[i]
        dk = dk_acc[hl, rows(b)] * SCALE
        dv = dv_acc[hl, rows(b)]
        if i == 0:
            arrived(dkv_got.at[hl], r_dkv.at[hl])
            dk = dk + dkv_got[hl, 0].astype(F32)
            dv = dv + dkv_got[hl, 1].astype(F32)
        dk_out[hl, rows(b)] = dk.astype(BF16)
        dv_out[hl, rows(b)] = dv.astype(BF16)
        give_back(dk_out, dk_res, 1, hl, b)
        give_back(dv_out, dv_res, 2, hl, b)

    def finish_queries(hl, i):
        b = order[i]
        arrived(dq_got.at[hl, rows(b)], r_d.at[hl, b])
        dq = dq_own[hl, rows(b)] + dq_got[hl, rows(b)].astype(F32)
        if i == BLOCKS - 1:
            dq = dq + dqe_got[hl, pl.ds(0, HALF)].astype(F32)
        dq_out[hl, rows(b)] = dq.astype(BF16)
        give_back(dq_out, dq_res, 0, hl, b)

    forward_edge(0)
    arrived(st.at[1], r_st.at[1])
    pending.append(remote(st.at[:, pl.ds(2 * eb, 2)], est, s_st2.at[1], r_st.at[2], near))
    forward_kv(0)
    for i in range(BLOCKS):
        queries(0, 0, i)
    for i in reversed(range(BLOCKS)):
        queries(0, 1, i)
    forward_kv(1)
    for i in (2, 1, 0):
        send_queries(0, i)
    for i in (2, 1):
        finish_keys(0, i)
    forward_edge(1)
    for i in range(BLOCKS):
        queries(1, 0, i)
    arrived(est, r_st.at[2])
    edge(0)
    send_edge_keys(0)
    finish_keys(0, 3)
    for i in (3, 2, 1, 0):
        queries(1, 1, i)
        if i < BLOCKS - 1:
            send_queries(1, i)
    for i in (2, 1):
        finish_keys(1, i)
    edge(1)
    send_edge_keys(1)
    finish_keys(1, 3)
    send_queries(0, 3)
    for i in (1, 2, 3):
        finish_queries(0, i)
    send_queries(1, 3)
    for i in (1, 2, 3):
        finish_queries(1, i)
    finish_keys(0, 0)
    finish_keys(1, 0)
    finish_queries(0, 0)
    finish_queries(1, 0)

    for copy in pending:
        copy.wait_send()
    for n in range(4):
        for hl in range(2):
            arrived(kv.at[0, 0, pl.ds(0, 7 * 128)], s_a.at[n, hl])
    for n, res in enumerate((dq_res, dk_res, dv_res)):
        arrived(dk_out.at[:, pl.ds(0, 7 * 128)], s_out.at[n])
        arrived(res, r_out.at[n])


def copy_kernel(a_ref, b_ref, c_ref, a_res, b_res, c_res, held, sems):
    refs = ((a_ref, a_res), (b_ref, b_res), (c_ref, c_res))
    loads = [pltpu.make_async_copy(src, held.at[n], sems.at[0, n]) for n, (src, _) in enumerate(refs)]
    stores = [pltpu.make_async_copy(held.at[n], dst, sems.at[1, n]) for n, (_, dst) in enumerate(refs)]
    for load in loads:
        load.start()
    for load, store in zip(loads, stores):
        load.wait()
        store.start()
    for store in stores:
        store.wait()


def per_device(queries, keys, values, outputs, out_grad, log_sum):
    groups = lax.axis_size("blk") // 2
    tokens, width = queries.shape
    any_ = pl.BlockSpec(memory_space=pl.ANY)
    dma = pltpu.SemaphoreType.DMA
    result = jax.ShapeDtypeStruct((tokens, width), BF16)
    scratch = [
        pltpu.VMEM((2, 2, 2, ROWS, HD), BF16),
        pltpu.VMEM((2, 2, ROWS, HD), BF16),
        pltpu.VMEM((2, 2, HALF, HD), BF16),
        pltpu.VMEM((2, 2, 2 * HALF, HD), BF16),
        pltpu.VMEM((8 * SLOTS, 128), F32),
        pltpu.VMEM((2, SLOTS, 8, 128), F32),
        pltpu.VMEM((2, 2, 8, 128), F32),
        pltpu.VMEM((tokens, width), BF16),
        pltpu.VMEM((tokens, width), BF16),
        pltpu.VMEM(log_sum.shape[::-1], F32),
        pltpu.VMEM((2, HALF, HD), F32),
        pltpu.VMEM((2, ROWS, HD), F32),
        pltpu.VMEM((2, ROWS, HD), F32),
        pltpu.VMEM((2, ROWS, HD), F32),
        pltpu.VMEM((2, ROWS, HD), BF16),
        pltpu.VMEM((2, ROWS, HD), BF16),
        pltpu.VMEM((2, ROWS, HD), BF16),
        pltpu.VMEM((2, ROWS, HD), BF16),
        pltpu.VMEM((2, ROWS, HD), BF16),
        pltpu.VMEM((2, 2 * HALF, HD), BF16),
        pltpu.VMEM((2, 2 * HALF, HD), BF16),
        pltpu.VMEM((2, 2, HALF, HD), BF16),
        pltpu.VMEM((2, 2, HALF, HD), BF16),
        dma((3,)),
        dma((2, SLOTS)),
        dma((2,)),
        dma((2, BLOCKS)),
        dma((2,)),
        dma((2,)),
        dma((3,)),
        dma((2,)),
        dma((2,)),
        dma((2, BLOCKS)),
        dma((3,)),
        dma((4, 2)),
        dma((2, SLOTS)),
        dma((2,)),
        dma((2, 2)),
        dma((SLOTS,)),
        dma((2,)),
        dma((2,)),
        dma((2,)),
        dma((2, BLOCKS)),
        dma((3,)),
    ]

    def body(*refs):
        kernel(groups, *refs)

    grads = pl.pallas_call(
        body,
        out_shape=(result, result, result),
        in_specs=[any_] * 6,
        out_specs=(any_, any_, any_),
        scratch_shapes=scratch,
        compiler_params=pltpu.CompilerParams(
            collective_id=0, has_side_effects=True, vmem_limit_bytes=60 * 2**20
        ),
        cost_estimate=pl.CostEstimate(flops=4 * 10**9, bytes_accessed=4 * 2**20, transcendentals=3 * 2**20),
        name="attention_backward",
    )(queries, keys, values, outputs, out_grad, jnp.transpose(log_sum))
    return pl.pallas_call(
        copy_kernel,
        out_shape=(result, result, result),
        in_specs=[any_] * 3,
        out_specs=(any_, any_, any_),
        scratch_shapes=[pltpu.VMEM((3, tokens, width), BF16), dma((2, 3))],
        compiler_params=pltpu.CompilerParams(vmem_limit_bytes=60 * 2**20),
        name="results",
    )(*grads)


def solution(mesh):
    spec = P(("blk", "head"), None)
    return jax.shard_map(
        per_device, mesh=mesh, in_specs=(spec,) * 6, out_specs=(spec,) * 3, check_vma=False
    )
```

time: 79.7 us -> 71.9 us (0.902)
  local copies, waits for them, and re-layouts: 3.97 us -> 0 us
  Pallas kernels: 74.8 us -> 71.1 us
    pallas_call x1, Pallas kernels: 74.8 us -> 68.9 us  [per_device(): pl.pallas_call(body, out_shape=(result, result, result), in_specs=[any_]...]
    unnamed x7 -> x0, local copies, waits for them, and re-layouts: 3.97 us -> none
    pallas_call x0 -> x1, Pallas kernels: none -> 2.23 us  [per_device(): pl.pallas_call(copy_kernel, out_shape=(result, result, result), in_specs=...]
where the time goes in v2:
time: 71.9 us; the launch traced here: 71.7 us
  Pallas kernels  71.1 us (99%)
    pallas_call x1, Pallas kernels, per_device(): pl.pallas_call(body, out_shape=(result, result, result), in_specs=[any_]...  68.9 us
    pallas_call x1, Pallas kernels, per_device(): pl.pallas_call(copy_kernel, out_shape=(result, result, result), in_specs=...  2.23 us

profile of v2, /device:TPU:1, one launch (start us, length us, event | category | flops | bytes accessed | tf_op | source)
XLA Modules:
  0.0 71.7 jit_solution(10941717595450256996)
XLA Ops:
  0.6 68.9 %attention_backward.1 = (bf16[128,2048]{1,0:T(8,128)(2,1)}, bf16[128,2048]{1,0:T(8,128)(2,1)}, bf16[128,2048]{1,0:T(8,128)(2,1)}) custom-call(bf16[128,2048]{1,0:T(8,128)(2,1)} %refs_0_.1, bf16[128,2048]{1,0:T(8,128)(2,1)} %refs_1_.1, bf16[128,2048]{1,0:T(8,128)(2,1)} %refs_2_.1, bf16[128,2048]{1,0:T(8,128)(2,1)} %refs_3_.1, bf16[128,2048]{1,0:T(8,128)(2,1)} %refs_4_.1, ...), custom_call_target="tpu_custom_call" | custom-call | flops 4000000000 | bytes 4194304 | tf_op jit(solution)/shard_map/attention_backward/pallas_call | solution.py:403
  69.5 2.2 %results.1 = (bf16[128,2048]{1,0:T(8,128)(2,1)}, bf16[128,2048]{1,0:T(8,128)(2,1)}, bf16[128,2048]{1,0:T(8,128)(2,1)}) custom-call(bf16[128,2048]{1,0:T(8,128)(2,1)} %get-tuple-element.6.a_ref, bf16[128,2048]{1,0:T(8,128)(2,1)} %get-tuple-element.7.b_ref, bf16[128,2048]{1,0:T(8,128)(2,1)} %get-tuple-element.8.c_ref), custom_call_target="tpu_custom_call" | custom-call | tf_op jit(solution)/shard_map/results/pallas_call | solution.py:415

commit v3 on v2

--- a/solution.py
+++ b/solution.py
@@ -135,7 +135,6 @@
     spread(0, 0, others)
     for hl in range(2):
         forward(hl, me_s)
-    spread(1, 0, others)
     twin_s = (1 - c) * NX + x
     for hl in range(2):
         forward(hl, twin_s)
@@ -164,17 +163,17 @@
             st.at[0, me_s], s_st.at[n], r_st.at[0], device_at(xt, ct),
         ))
 
+    spread(0, 1, twin + others)
+
     rest = [cc * NX + lax.rem(x + dx, NX) for dx in (3, 1, 2) for cc in range(2)]
-    for s in rest:
+    for s in rest[:4]:
         forward(0, s)
-    spread(0, 1, twin + others)
-    spread(1, 1, twin + others)
-    for s in rest[:4]:
-        forward(1, s)
+    spread(1, 0, others)
     arrived(st.at[0], r_st.at[0])
     pending.append(remote(st.at[0], st.at[1], s_st2.at[0], r_st.at[1], partner))
     for s in rest[4:]:
-        forward(1, s)
+        forward(0, s)
+    spread(1, 1, twin + others)
 
     dk_acc[...] = jnp.zeros_like(dk_acc)
     dv_acc[...] = jnp.zeros_like(dv_acc)
@@ -183,10 +182,12 @@
         arrived(kv.at[:, hl], r_kv.at[hl])
         pending.append(remote(kv.at[:, hl, rows(pb)], kvp.at[hl], s_k.at[hl], r_k.at[hl], partner))
 
-    def forward_edge(hl):
+    def forward_own_edge(hl):
         pending.append(remote(
             qg.at[0, :, hl, rows(eb)], eqg.at[hl, :, pl.ds(0, HALF)], s_c.at[hl, 0], r_c.at[hl], near
         ))
+
+    def forward_edge(hl):
         arrived(qg.at[1, :, hl, rows(eb)], r_b.at[hl, eb])
         pending.append(remote(
             qg.at[1, :, hl, rows(eb)], eqg.at[hl, :, pl.ds(HALF, HALF)], s_c.at[hl, 1], r_c.at[hl], near
@@ -281,44 +282,52 @@
         dq_out[hl, rows(b)] = dq.astype(BF16)
         give_back(dq_out, dq_res, 0, hl, b)
 
+    forward_own_edge(0)
+    forward_kv(0)
+    for i in range(BLOCKS):
+        queries(0, 0, i)
+    for s in rest[:4]:
+        forward(1, s)
     forward_edge(0)
     arrived(st.at[1], r_st.at[1])
     pending.append(remote(st.at[:, pl.ds(2 * eb, 2)], est, s_st2.at[1], r_st.at[2], near))
-    forward_kv(0)
-    for i in range(BLOCKS):
-        queries(0, 0, i)
-    for i in reversed(range(BLOCKS)):
+    for i in (3, 2):
         queries(0, 1, i)
+    for s in rest[4:]:
+        forward(1, s)
+    forward_own_edge(1)
+    for i in (1, 0):
+        queries(0, 1, i)
+    arrived(est, r_st.at[2])
+    edge(0)
+    for i in (2, 1, 3):
+        finish_keys(0, i)
+    forward_edge(1)
     forward_kv(1)
     for i in (2, 1, 0):
         send_queries(0, i)
-    for i in (2, 1):
-        finish_keys(0, i)
-    forward_edge(1)
+    send_edge_keys(0)
     for i in range(BLOCKS):
         queries(1, 0, i)
-    arrived(est, r_st.at[2])
-    edge(0)
-    send_edge_keys(0)
-    finish_keys(0, 3)
-    for i in (3, 2, 1, 0):
+    send_queries(0, 3)
+    for i in (3, 2):
         queries(1, 1, i)
-        if i < BLOCKS - 1:
-            send_queries(1, i)
-    for i in (2, 1):
-        finish_keys(1, i)
     edge(1)
     send_edge_keys(1)
-    finish_keys(1, 3)
-    send_queries(0, 3)
+    send_queries(1, 2)
+    for i in (1, 0):
+        queries(1, 1, i)
+        send_queries(1, i)
+    for i in (2, 1, 3):
+        finish_keys(1, i)
     for i in (1, 2, 3):
         finish_queries(0, i)
+    finish_keys(0, 0)
     send_queries(1, 3)
+    finish_queries(0, 0)
+    finish_keys(1, 0)
     for i in (1, 2, 3):
         finish_queries(1, i)
-    finish_keys(0, 0)
-    finish_keys(1, 0)
-    finish_queries(0, 0)
     finish_queries(1, 0)
 
     for copy in pending:

time: 71.9 us -> 69.6 us (0.968); the launches traced: 71.7 us -> 68.5 us
  Pallas kernels: 71.1 us -> 67.9 us
    pallas_call x1, Pallas kernels: 68.9 us -> 65.6 us  [per_device(): pl.pallas_call(body, out_shape=(result, result, result), in_specs=[any_]...]
where the time goes in v3:
time: 69.6 us; the launch traced here: 68.5 us
  Pallas kernels  67.9 us (98%)
    pallas_call x1, Pallas kernels, per_device(): pl.pallas_call(body, out_shape=(result, result, result), in_specs=[any_]...  65.6 us
    pallas_call x1, Pallas kernels, per_device(): pl.pallas_call(copy_kernel, out_shape=(result, result, result), in_specs=...  2.23 us

profile of v3, /device:TPU:1, one launch (start us, length us, event | category | flops | bytes accessed | tf_op | source)
XLA Modules:
  0.0 68.5 jit_solution(8453744453444733573)
XLA Ops:
  0.6 65.6 %attention_backward.1 = (bf16[128,2048]{1,0:T(8,128)(2,1)}, bf16[128,2048]{1,0:T(8,128)(2,1)}, bf16[128,2048]{1,0:T(8,128)(2,1)}) custom-call(bf16[128,2048]{1,0:T(8,128)(2,1)} %refs_0_.1, bf16[128,2048]{1,0:T(8,128)(2,1)} %refs_1_.1, bf16[128,2048]{1,0:T(8,128)(2,1)} %refs_2_.1, bf16[128,2048]{1,0:T(8,128)(2,1)} %refs_3_.1, bf16[128,2048]{1,0:T(8,128)(2,1)} %refs_4_.1, ...), custom_call_target="tpu_custom_call" | custom-call | flops 4000000000 | bytes 4194304 | tf_op jit(solution)/shard_map/attention_backward/pallas_call | solution.py:412
  66.3 2.2 %results.1 = (bf16[128,2048]{1,0:T(8,128)(2,1)}, bf16[128,2048]{1,0:T(8,128)(2,1)}, bf16[128,2048]{1,0:T(8,128)(2,1)}) custom-call(bf16[128,2048]{1,0:T(8,128)(2,1)} %get-tuple-element.6.a_ref, bf16[128,2048]{1,0:T(8,128)(2,1)} %get-tuple-element.7.b_ref, bf16[128,2048]{1,0:T(8,128)(2,1)} %get-tuple-element.8.c_ref), custom_call_target="tpu_custom_call" | custom-call | tf_op jit(solution)/shard_map/results/pallas_call | solution.py:424

commit v4 on v3

--- a/solution.py
+++ b/solution.py
@@ -49,7 +49,7 @@
     dq_edge, dq_own, dk_acc, dv_acc,
     dq_oth, dq_got, dq_out, dk_out, dv_out, dqe_out, dqe_got, dkv_out, dkv_got,
     loc, r_qg, r_kv, r_b, r_k, r_c, r_st, r_dqe, r_dkv, r_d, r_out,
-    s_a, s_b, s_k, s_c, s_st, s_st2, s_dqe, s_dkv, s_d, s_out,
+    s_a, s_b, s_k, s_c, s_st, s_st2, s_dqe, s_dkv, s_d, s_out, s_dl, r_dl,
 ):
     head = lax.axis_index("head")
     blk = lax.axis_index("blk")
@@ -130,11 +130,11 @@
             qg.at[0, :, hl, run(s)], qg.at[1, :, hl, run(s)], s_b.at[hl, s], r_b.at[hl, lax.div(s, 2)], partner
         ))
 
+    forward(0, me_s)
     spread(0, 0, twin)
+    spread(0, 0, others)
     spread(1, 0, twin)
-    spread(0, 0, others)
-    for hl in range(2):
-        forward(hl, me_s)
+    forward(1, me_s)
     twin_s = (1 - c) * NX + x
     for hl in range(2):
         forward(hl, twin_s)
@@ -242,12 +242,18 @@
         if i == BLOCKS - 1:
             arrived(dqe_got.at[hl], r_dqe.at[hl])
             dq_oth[hl, rows(b)] = (dq_edge[hl] + dqe_got[hl, pl.ds(HALF, HALF)].astype(F32)).astype(BF16)
-        pending.append(remote(
-            dq_oth.at[hl, rows(b)], dq_got.at[hl, rows(b)], s_d.at[hl, b], r_d.at[hl, b], partner
-        ))
-
-    def give_back(buf, res, n, hl, b):
-        for j in range(2):
+        if hl == 1 and i == BLOCKS - 1:
+            for j in range(2):
+                pending.append(remote(
+                    dq_oth.at[hl, run(2 * b + j)], dq_got.at[hl, run(2 * b + j)], s_dl.at[j], r_dl.at[j], partner
+                ))
+        else:
+            pending.append(remote(
+                dq_oth.at[hl, rows(b)], dq_got.at[hl, rows(b)], s_d.at[hl, b], r_d.at[hl, b], partner
+            ))
+
+    def give_back(buf, res, n, hl, b, runs=(0, 1)):
+        for j in runs:
             s = 2 * b + j
             src = buf.at[hl, run(s)]
             dst = res.at[:, cols(me_t, hl)]
@@ -272,6 +278,13 @@
         dv_out[hl, rows(b)] = dv.astype(BF16)
         give_back(dk_out, dk_res, 1, hl, b)
         give_back(dv_out, dv_res, 2, hl, b)
+
+    def finish_last():
+        for j in range(2):
+            s = 2 * order[0] + j
+            arrived(dq_got.at[1, run(s)], r_dl.at[j])
+            dq_out[1, run(s)] = (dq_own[1, run(s)] + dq_got[1, run(s)].astype(F32)).astype(BF16)
+            give_back(dq_out, dq_res, 0, 1, order[0], (j,))
 
     def finish_queries(hl, i):
         b = order[i]
@@ -302,9 +315,10 @@
     edge(0)
     for i in (2, 1, 3):
         finish_keys(0, i)
+    send_queries(0, 2)
     forward_edge(1)
     forward_kv(1)
-    for i in (2, 1, 0):
+    for i in (1, 0):
         send_queries(0, i)
     send_edge_keys(0)
     for i in range(BLOCKS):
@@ -328,7 +342,7 @@
     finish_keys(1, 0)
     for i in (1, 2, 3):
         finish_queries(1, i)
-    finish_queries(1, 0)
+    finish_last()
 
     for copy in pending:
         copy.wait_send()
@@ -404,6 +418,8 @@
         dma((2,)),
         dma((2, BLOCKS)),
         dma((3,)),
+        dma((2,)),
+        dma((2,)),
     ]
 
     def body(*refs):

time: 69.6 us -> 69.3 us (level); the launches traced: 68.5 us -> 69.2 us
    pallas_call x1, Pallas kernels: 65.6 us -> 66.3 us  [per_device(): pl.pallas_call(body, out_shape=(result, result, result), in_specs=[any_]...]
where the time goes in v4:
time: 69.3 us; the launch traced here: 69.2 us
  Pallas kernels  68.5 us (99%)
    pallas_call x1, Pallas kernels, per_device(): pl.pallas_call(body, out_shape=(result, result, result), in_specs=[any_]...  66.3 us
    pallas_call x1, Pallas kernels, per_device(): pl.pallas_call(copy_kernel, out_shape=(result, result, result), in_specs=...  2.23 us

profile of v4, /device:TPU:1, one launch (start us, length us, event | category | flops | bytes accessed | tf_op | source)
XLA Modules:
  0.0 69.2 jit_solution(986994911955021548)
XLA Ops:
  0.6 66.3 %attention_backward.1 = (bf16[128,2048]{1,0:T(8,128)(2,1)}, bf16[128,2048]{1,0:T(8,128)(2,1)}, bf16[128,2048]{1,0:T(8,128)(2,1)}) custom-call(bf16[128,2048]{1,0:T(8,128)(2,1)} %refs_0_.1, bf16[128,2048]{1,0:T(8,128)(2,1)} %refs_1_.1, bf16[128,2048]{1,0:T(8,128)(2,1)} %refs_2_.1, bf16[128,2048]{1,0:T(8,128)(2,1)} %refs_3_.1, bf16[128,2048]{1,0:T(8,128)(2,1)} %refs_4_.1, ...), custom_call_target="tpu_custom_call" | custom-call | flops 4000000000 | bytes 4194304 | tf_op jit(solution)/shard_map/attention_backward/pallas_call | solution.py:428
  67.0 2.2 %results.1 = (bf16[128,2048]{1,0:T(8,128)(2,1)}, bf16[128,2048]{1,0:T(8,128)(2,1)}, bf16[128,2048]{1,0:T(8,128)(2,1)}) custom-call(bf16[128,2048]{1,0:T(8,128)(2,1)} %get-tuple-element.6.a_ref, bf16[128,2048]{1,0:T(8,128)(2,1)} %get-tuple-element.7.b_ref, bf16[128,2048]{1,0:T(8,128)(2,1)} %get-tuple-element.8.c_ref), custom_call_target="tpu_custom_call" | custom-call | tf_op jit(solution)/shard_map/results/pallas_call | solution.py:440

commit v5 on v4

--- a/solution.py
+++ b/solution.py
@@ -324,16 +324,15 @@
     for i in range(BLOCKS):
         queries(1, 0, i)
     send_queries(0, 3)
-    for i in (3, 2):
+    for i in (3, 2, 1, 0):
         queries(1, 1, i)
+    for i in (2, 1):
+        finish_keys(1, i)
     edge(1)
     send_edge_keys(1)
-    send_queries(1, 2)
-    for i in (1, 0):
-        queries(1, 1, i)
+    for i in (2, 1, 0):
         send_queries(1, i)
-    for i in (2, 1, 3):
-        finish_keys(1, i)
+    finish_keys(1, 3)
     for i in (1, 2, 3):
         finish_queries(0, i)
     finish_keys(0, 0)

time: 69.3 us -> 68.1 us (0.983)
  the two profiles are of different devices: /device:TPU:1 before, /device:TPU:7 now
where the time goes in v5:
time: 68.1 us; the launch traced here: 68 us
  Pallas kernels  67.3 us (99%)
    pallas_call x1, Pallas kernels, per_device(): pl.pallas_call(body, out_shape=(result, result, result), in_specs=[any_]...  65.1 us
    pallas_call x1, Pallas kernels, per_device(): pl.pallas_call(copy_kernel, out_shape=(result, result, result), in_specs=...  2.23 us

profile of v5, /device:TPU:7, one launch (start us, length us, event | category | flops | bytes accessed | tf_op | source)
XLA Modules:
  0.0 68.0 jit_solution(7877926816821522426)
XLA Ops:
  0.6 65.1 %attention_backward.1 = (bf16[128,2048]{1,0:T(8,128)(2,1)}, bf16[128,2048]{1,0:T(8,128)(2,1)}, bf16[128,2048]{1,0:T(8,128)(2,1)}) custom-call(bf16[128,2048]{1,0:T(8,128)(2,1)} %refs_0_.1, bf16[128,2048]{1,0:T(8,128)(2,1)} %refs_1_.1, bf16[128,2048]{1,0:T(8,128)(2,1)} %refs_2_.1, bf16[128,2048]{1,0:T(8,128)(2,1)} %refs_3_.1, bf16[128,2048]{1,0:T(8,128)(2,1)} %refs_4_.1, ...), custom_call_target="tpu_custom_call" | custom-call | flops 4000000000 | bytes 4194304 | tf_op jit(solution)/shard_map/attention_backward/pallas_call | solution.py:427
  65.7 2.2 %results.1 = (bf16[128,2048]{1,0:T(8,128)(2,1)}, bf16[128,2048]{1,0:T(8,128)(2,1)}, bf16[128,2048]{1,0:T(8,128)(2,1)}) custom-call(bf16[128,2048]{1,0:T(8,128)(2,1)} %get-tuple-element.6.a_ref, bf16[128,2048]{1,0:T(8,128)(2,1)} %get-tuple-element.7.b_ref, bf16[128,2048]{1,0:T(8,128)(2,1)} %get-tuple-element.8.c_ref), custom_call_target="tpu_custom_call" | custom-call | tf_op jit(solution)/shard_map/results/pallas_call | solution.py:439
